TPU v7x, 32 devices: a whole 2x2x4 slice. The times are simulated.
32 devices in a mesh: outer: 4 (over x, core), inner: 8 (over z, y).
Axes of the slice: x: 2, y: 2, z: 4, core: 2. Of those that a mesh axis runs over, the one named last changes fastest.
Arguments:
- queue: bfloat16 [131072, 512], P(('outer', 'inner')), may hold values from -100 to 100
- pred: bfloat16 [4096, 512], P(('outer', 'inner')), may hold values from -1 to 1
- owner: int32 [4096, 1], P(('outer', 'inner')), may hold values from 0 to 31, as said below
- slot: int32 [4096], P(('outer', 'inner')), may hold values from 0 to 4095
Outputs:
- grad_pred: float32 [4096, 512], P(('outer', 'inner'))
Inputs may be any that keep to these rules, and one draw needn't show every extreme that they name: Queue shard o lies on the device of outer index o // 8 and inner index o % 8. Among the rows of one device (aligned blocks of 128 rows), at most 32 name owners of one inner index; among the rows of one outer group (aligned blocks of 1024 rows), at most 64 name the same owner.
All inputs are finite; a program needn't handle non-finite values.
Results may differ from a plain program's by a relative error of at most 0.012.
Values may be sent and summed in bfloat16 or wider, within the bound.
A program may use at most 128 MiB of HBM per device.

v0:
```python
import jax
import jax.numpy as jnp
from jax import lax
from jax.sharding import PartitionSpec as P

EPS = 1e-06
INV_TAU = 10.0


def block_exp(row_block, column_block):
    return jnp.exp(
        jnp.einsum("rd,cd->rc", row_block, column_block, preferred_element_type=jnp.float32)
        * INV_TAU
    )


def mixed_weights(exponent, row_total, column_total, row_first, column_first, rows_dev):
    row_offset = jnp.arange(exponent.shape[0], dtype=jnp.int32)[:, None] - row_first
    column_offset = jnp.arange(exponent.shape[1], dtype=jnp.int32)[None, :] - column_first
    diagonal = ((row_offset == column_offset) & (row_offset >= 0) & (row_offset < rows_dev)).astype(
        jnp.float32
    )
    return (
        0.5 * (exponent / row_total[:, None] + exponent / column_total[None, :]) - diagonal
    ).astype(jnp.bfloat16)


def column_terms(weights, row_block):
    return lax.dot_general(
        weights, row_block, (((0,), (0,)), ((), ())), preferred_element_type=jnp.float32
    )


def shards(queue, pred, owner, slot):
    outer_count = lax.axis_size("outer")
    inner_count = lax.axis_size("inner")
    rows_dev = pred.shape[0]
    feature_width = queue.shape[1]
    cap_member = max(2, 2 * rows_dev // inner_count)
    cap_group = inner_count * cap_member // outer_count
    owners_of = owner[:, 0]
    owner_member = owners_of % inner_count
    owner_group = owners_of // inner_count
    position = jnp.arange(rows_dev, dtype=jnp.int32)
    earlier = (owner_member[:, None] == owner_member[None, :]) & (
        position[None, :] < position[:, None]
    )
    member_place = owner_member * cap_member + jnp.sum(earlier.astype(jnp.int32), 1)
    request_slot = jnp.full((inner_count * cap_member,), -1, jnp.int32).at[member_place].set(slot)
    request_group = (
        jnp.full((inner_count * cap_member,), outer_count, jnp.int32)
        .at[member_place]
        .set(owner_group)
    )
    request_slot = request_slot.reshape(inner_count, cap_member)
    request_group = request_group.reshape(inner_count, cap_member)
    relay_slot, relay_group = (
        lax.all_to_all(request_slot, "inner", split_axis=0, concat_axis=0, tiled=True),
        lax.all_to_all(request_group, "inner", split_axis=0, concat_axis=0, tiled=True),
    )
    relay_slot = relay_slot.reshape(-1)
    relay_group = relay_group.reshape(-1)
    entry_index = jnp.arange(relay_slot.shape[0], dtype=jnp.int32)
    ahead = (relay_group[:, None] == relay_group[None, :]) & (
        entry_index[None, :] < entry_index[:, None]
    )
    group_place = relay_group * cap_group + jnp.sum(ahead.astype(jnp.int32), 1)
    asking = (
        jnp.full((outer_count * cap_group,), -1, jnp.int32)
        .at[group_place]
        .set(relay_slot, mode="drop")
    )
    asking = asking.reshape(outer_count, cap_group)
    asked = lax.all_to_all(asking, "outer", split_axis=0, concat_axis=0, tiled=True)
    looked = jnp.take(queue, jnp.maximum(asked, 0), axis=0)
    looked = jnp.where((asked >= 0)[..., None], looked, jnp.zeros((), jnp.bfloat16))
    answered = lax.all_to_all(looked, "outer", split_axis=0, concat_axis=0, tiled=True)
    answered = answered.reshape(outer_count * cap_group, feature_width)
    relayed = jnp.take(answered, jnp.minimum(group_place, outer_count * cap_group - 1), axis=0)
    relayed = jnp.where((relay_slot >= 0)[:, None], relayed, jnp.zeros((), jnp.bfloat16))
    relayed = relayed.reshape(inner_count, cap_member, feature_width)
    returned = lax.all_to_all(relayed, "inner", split_axis=0, concat_axis=0, tiled=True)
    fetched = jnp.take(
        returned.reshape(inner_count * cap_member, feature_width), member_place, axis=0
    ).astype(jnp.float32)
    neighbour = (fetched * lax.rsqrt(jnp.sum(fetched * fetched, 1, keepdims=True) + EPS)).astype(
        jnp.bfloat16
    )
    predicted = pred.astype(jnp.float32)
    inverse = lax.rsqrt(jnp.sum(predicted * predicted, 1, keepdims=True) + EPS)
    queries = (predicted * inverse).astype(jnp.bfloat16)
    outer_at = lax.axis_index("outer")
    inner_at = lax.axis_index("inner")
    row_block = lax.all_gather(neighbour, "inner", axis=0, tiled=True)
    exponent = block_exp(row_block, lax.all_gather(queries, "outer", axis=0, tiled=True))
    row_total = lax.psum(jnp.sum(exponent, 1), "inner")
    column_total = lax.psum(jnp.sum(exponent, 0), "outer")
    weights = mixed_weights(
        exponent, row_total, column_total, inner_at * rows_dev, outer_at * rows_dev, rows_dev
    )
    dquery = lax.psum_scatter(
        column_terms(weights, row_block), "outer", scatter_dimension=0, tiled=True
    )
    dquery = dquery * INV_TAU
    radial = jnp.sum(predicted * dquery, 1, keepdims=True)
    return inverse * dquery - predicted * inverse * inverse * inverse * radial


def solution(mesh):
    in_specs = (
        P(("outer", "inner"), None),
        P(("outer", "inner"), None),
        P(("outer", "inner"), None),
        P(("outer", "inner")),
    )
    out_specs = P(("outer", "inner"), None)
    return jax.shard_map(shards, mesh=mesh, in_specs=in_specs, out_specs=out_specs, check_vma=False)
```

profile of v0, /device:TPU:0, one launch (start us, length us, event | category | flops | bytes accessed | tf_op | source)
XLA Modules:
  0.0 176.9 jit_solution(1068973919540385708)
XLA Ops:
  8.7 1.0 scatter_custom_fusion.1
  10.4 7.3 %all-to-all-start.1 = ((s32[8,1,32]{2,1,0:T(1,128)}), s32[8,1,32]{2,1,0:T(1,128)S(1)}, u32[]{:S(2)}, u32[]{:S(2)}) async-start(s32[8,1,32]{2,1,0:T(1,128)} %all_to_all.26), calls=%async_computation.1 | async-start | bytes 8192 | tf_op jit(solution)/shard_map/all_to_all | solution.py:59
  17.7 1.1 scatter_custom_fusion
  19.4 4.6 %all-to-all-done.1 = s32[8,1,32]{2,1,0:T(1,128)S(1)} async-done(((s32[8,1,32]{2,1,0:T(1,128)}), s32[8,1,32]{2,1,0:T(1,128)S(1)}, u32[]{:S(2)}, u32[]{:S(2)}) %all-to-all-start.1) | async-done | bytes 1056 | tf_op jit(solution)/shard_map/all_to_all | solution.py:59
  24.0 3.3 %all-to-all-start = ((s32[8,1,32]{2,1,0:T(1,128)}), s32[8,1,32]{2,1,0:T(1,128)S(1)}, u32[]{:S(2)}, u32[]{:S(2)}) async-start(s32[8,1,32]{2,1,0:T(1,128)} %all_to_all.24), calls=%async_computation | async-start | bytes 8192 | tf_op jit(solution)/shard_map/all_to_all | solution.py:58
  29.0 4.8 %all-to-all-done = s32[8,1,32]{2,1,0:T(1,128)S(1)} async-done(((s32[8,1,32]{2,1,0:T(1,128)}), s32[8,1,32]{2,1,0:T(1,128)S(1)}, u32[]{:S(2)}, u32[]{:S(2)}) %all-to-all-start) | async-done | bytes 1056 | tf_op jit(solution)/shard_map/all_to_all | solution.py:58
  34.5 1.4 scatter_custom_fusion.2
  36.6 3.2 %all-to-all-start.2 = ((s32[4,1,64]{2,1,0:T(1,128)}), s32[4,1,64]{2,1,0:T(1,128)S(1)}, u32[]{:S(2)}, u32[]{:S(2)}) async-start(s32[4,1,64]{2,1,0:T(1,128)} %all_to_all.28), calls=%async_computation.2 | async-start | bytes 4096 | tf_op jit(solution)/shard_map/all_to_all | solution.py:74
  39.9 3.6 %all-to-all-done.2 = s32[4,1,64]{2,1,0:T(1,128)S(1)} async-done(((s32[4,1,64]{2,1,0:T(1,128)}), s32[4,1,64]{2,1,0:T(1,128)S(1)}, u32[]{:S(2)}, u32[]{:S(2)}) %all-to-all-start.2) | async-done | bytes 1056 | tf_op jit(solution)/shard_map/all_to_all | solution.py:74
  43.6 3.9 %gather_fusion = bf16[256,512]{1,0:T(8,128)(2,1)S(1)} fusion(bf16[4096,512]{1,0:T(8,128)(2,1)} %param.4, s32[1024]{0:T(1024)S(1)} %pad_clamp_fusion.2), kind=kCustom, calls=%fused_computation | custom fusion | bytes 525312 | tf_op jit(solution)/shard_map/jit(_take)/gather | solution.py:75
  48.4 3.4 %all-to-all-start.3 = ((bf16[4,64,512]{2,1,0:T(8,128)(2,1)}), bf16[4,64,512]{2,1,0:T(8,128)(2,1)S(1)}, u32[]{:S(2)}, u32[]{:S(2)}) async-start(bf16[4,64,512]{2,1,0:T(8,128)(2,1)} %select_select_fusion.1), calls=%async_computation.3 | async-start | bytes 524288 | tf_op jit(solution)/shard_map/all_to_all | solution.py:77
  51.8 6.0 %all-to-all-done.3 = bf16[4,64,512]{2,1,0:T(8,128)(2,1)S(1)} async-done(((bf16[4,64,512]{2,1,0:T(8,128)(2,1)}), bf16[4,64,512]{2,1,0:T(8,128)(2,1)S(1)}, u32[]{:S(2)}, u32[]{:S(2)}) %all-to-all-start.3) | async-done | bytes 262176 | tf_op jit(solution)/shard_map/all_to_all | solution.py:77
  57.8 1.2 gather_fusion.1
  59.8 3.4 %all-to-all-start.4 = ((bf16[8,32,512]{2,1,0:T(8,128)(2,1)}), bf16[8,32,512]{2,1,0:T(8,128)(2,1)S(1)}, u32[]{:S(2)}, u32[]{:S(2)}) async-start(bf16[8,32,512]{2,1,0:T(8,128)(2,1)} %select_select_fusion), calls=%async_computation.4 | async-start | bytes 524288 | tf_op jit(solution)/shard_map/all_to_all | solution.py:82
  63.3 8.9 %all-to-all-done.4 = bf16[8,32,512]{2,1,0:T(8,128)(2,1)S(1)} async-done(((bf16[8,32,512]{2,1,0:T(8,128)(2,1)}), bf16[8,32,512]{2,1,0:T(8,128)(2,1)S(1)}, u32[]{:S(2)}, u32[]{:S(2)}) %all-to-all-start.4) | async-done | bytes 262176 | tf_op jit(solution)/shard_map/all_to_all | solution.py:82
  74.4 6.5 %all_gather.7 = bf16[512,512]{1,0:T(8,128)(2,1)S(1)} all-gather(bf16[128,512]{1,0:T(8,128)(2,1)S(1)} %fusion.2), channel_id=1, replica_groups=mesh['outer'=4,'inner'=8] {'outer'}, dimensions={0}, use_global_device_ids=true | all-gather | bytes 655360 | tf_op jit(solution)/shard_map/all_gather | solution.py:95
  80.9 31.6 %all-gather.2.cloned.1.call-done = bf16[1024,512]{1,0:T(8,128)(2,1)} async-done(((bf16[128,512]{1,0:T(8,128)(2,1)}), bf16[1024,512]{1,0:T(8,128)(2,1)}) %all-gather.2.cloned.1.call-update) | async-done | bytes 1048592 | tf_op jit(solution)/shard_map/all_gather | solution.py:94
  112.4 3.5 %fusion.23 = (f32[1024]{0:T(1024)S(1)}, f32[512]{0:T(512)S(1)}, f32[1024,512]{1,0:T(8,128)}) fusion(bf16[1024,512]{1,0:T(8,128)(2,1)} %all-gather.2.cloned.1.call-done, bf16[512,512]{1,0:T(8,128)(2,1)S(1)} %all_gather.7), kind=kOutput, calls=%fused_computation.74 | convolution fusion | flops 538442240 | bytes 3676160 | tf_op jit(solution)/shard_map/rd,cd->rc/dot_general | solution.py:12
  115.9 19.2 %psum.14 = f32[1024]{0:T(1024)S(1)} all-reduce(f32[1024]{0:T(1024)S(1)} %get-tuple-element.5), channel_id=1, replica_groups=mesh['outer'=4,'inner'=8] {'inner'}, use_global_device_ids=true, to_apply=%region_8.9 | all-reduce | flops 1024 | bytes 8192 | tf_op jit(solution)/shard_map/psum | solution.py:96
  135.1 5.7 %psum.15 = f32[512]{0:T(512)S(1)} all-reduce(f32[512]{0:T(512)S(1)} %get-tuple-element.6), channel_id=1, replica_groups=mesh['outer'=4,'inner'=8] {'outer'}, use_global_device_ids=true, to_apply=%region_10.11 | all-reduce | flops 512 | bytes 4096 | tf_op jit(solution)/shard_map/psum | solution.py:97
  140.7 3.9 %fusion = f32[512,512]{1,0:T(8,128)} fusion(bf16[1024,512]{1,0:T(8,128)(2,1)S(1)} %copy-done.1, f32[1024,512]{1,0:T(8,128)} %get-tuple-element.20, s32[512]{0:T(512)S(1)} %iota_subtract_fusion.1, f32[512]{0:T(512)S(1)} %psum.15, f32[1024]{0:T(1024)S(1)} %psum.14, s32[1024]{0:T(1024)S(1)} %iota_subtract_fusion, pred[1024]{0:T(1024)(128)(4,1)S(1)} %get-tuple-element.23, ...), kind=kOutput, calls=%fused_computation.8 | convolution fusion | flops 542113792 | bytes 4208640 | tf_op jit(solution)/shard_map/dot_general | solution.py:29
  144.7 22.5 %reduce-scatter.2.cloned.1.call-done = f32[128,512]{1,0:T(8,128)} async-done(((f32[512,512]{1,0:T(8,128)}), f32[128,512]{1,0:T(8,128)}) %reduce-scatter.2.cloned.1.call-update) | async-done | bytes 262160 | tf_op jit(solution)/shard_map/reduce_scatter | solution.py:101
  167.2 1.1 fusion.9
  168.3 1.8 %fusion.5 = f32[128,512]{1,0:T(8,128)} fusion(bf16[128,512]{1,0:T(8,128)(2,1)S(1)} %copy-done, f32[128,512]{1,0:T(8,128)} %reduce-scatter.2.cloned.1.call-done, f32[128]{0:T(128)S(1)} %fusion.9, f32[128]{0:T(128)S(1)} %get-tuple-element.16, f32[128]{0:T(128)S(1)} %get-tuple-element.17), kind=kLoop, calls=%fused_computation.18 | loop fusion | flops 458752 | bytes 656896 | tf_op jit(solution)/shard_map/sub | solution.py:106
  (45 shorter events, 10.5 us)
Async XLA Ops:
  10.4 13.7 %all-to-all-start.1 = ((s32[8,1,32]{2,1,0:T(1,128)}), s32[8,1,32]{2,1,0:T(1,128)S(1)}, u32[]{:S(2)}, u32[]{:S(2)}) async-start(s32[8,1,32]{2,1,0:T(1,128)} %all_to_all.26), calls=%async_computation.1 | async-start | bytes 8192 | tf_op jit(solution)/shard_map/all_to_all | solution.py:59
  24.0 9.7 %all-to-all-start = ((s32[8,1,32]{2,1,0:T(1,128)}), s32[8,1,32]{2,1,0:T(1,128)S(1)}, u32[]{:S(2)}, u32[]{:S(2)}) async-start(s32[8,1,32]{2,1,0:T(1,128)} %all_to_all.24), calls=%async_computation | async-start | bytes 8192 | tf_op jit(solution)/shard_map/all_to_all | solution.py:58
  36.6 6.9 %all-to-all-start.2 = ((s32[4,1,64]{2,1,0:T(1,128)}), s32[4,1,64]{2,1,0:T(1,128)S(1)}, u32[]{:S(2)}, u32[]{:S(2)}) async-start(s32[4,1,64]{2,1,0:T(1,128)} %all_to_all.28), calls=%async_computation.2 | async-start | bytes 4096 | tf_op jit(solution)/shard_map/all_to_all | solution.py:74
  48.4 9.4 %all-to-all-start.3 = ((bf16[4,64,512]{2,1,0:T(8,128)(2,1)}), bf16[4,64,512]{2,1,0:T(8,128)(2,1)S(1)}, u32[]{:S(2)}, u32[]{:S(2)}) async-start(bf16[4,64,512]{2,1,0:T(8,128)(2,1)} %select_select_fusion.1), calls=%async_computation.3 | async-start | bytes 524288 | tf_op jit(solution)/shard_map/all_to_all | solution.py:77
  57.8 16.3 %copy-start = (bf16[128,512]{1,0:T(8,128)(2,1)S(1)}, bf16[128,512]{1,0:T(8,128)(2,1)}, u32[]{:S(2)}) copy-start(bf16[128,512]{1,0:T(8,128)(2,1)} %param.5) | copy-start | bytes 393220
  59.8 12.4 %all-to-all-start.4 = ((bf16[8,32,512]{2,1,0:T(8,128)(2,1)}), bf16[8,32,512]{2,1,0:T(8,128)(2,1)S(1)}, u32[]{:S(2)}, u32[]{:S(2)}) async-start(bf16[8,32,512]{2,1,0:T(8,128)(2,1)} %select_select_fusion), calls=%async_computation.4 | async-start | bytes 524288 | tf_op jit(solution)/shard_map/all_to_all | solution.py:82
  63.2 49.2 %all-gather.2.cloned.1.call-start = ((), (), s32[]{:S(2)}) async-start(), calls=%async_computation.6 | async-start | bytes 1179648 | tf_op jit(solution)/shard_map/all_gather | solution.py:94
  74.0 93.2 %reduce-scatter.2.cloned.1.call-start = ((), (), s32[]{:S(2)}) async-start(), calls=%async_computation.7 | async-start | bytes 1310720 | tf_op jit(solution)/shard_map/reduce_scatter | solution.py:101
  112.4 28.3 %copy-start.1 = (bf16[1024,512]{1,0:T(8,128)(2,1)S(1)}, bf16[1024,512]{1,0:T(8,128)(2,1)}, u32[]{:S(2)}) copy-start(bf16[1024,512]{1,0:T(8,128)(2,1)} %all-gather.2.cloned.1.call-done) | copy-start | bytes 3145732
Sparse Core Ops, SparseCore 0:
  74.1 38.2 all-gather.1
  144.8 22.3 reduce-scatter.1
where the time goes:
time: 178 us; the launch traced here: 177 us
  waiting for transfers between devices  82 us (46%)
  blocking collectives  31.3 us (18%)
  starting transfers between devices  20.7 us (12%)
  between operations  13.6 us (8%)
  local copies, waits for them, and re-layouts  12.3 us (7%)
  other arithmetic  9.5 us (5%)
  matrix products  7.41 us (4%)
    all_gather x1, waiting for transfers between devices, shards(): row_block = lax.all_gather(neighbour, 'inner', axis=0, tiled=True)  31.6 us
    reduce_scatter x1, waiting for transfers between devices, shards(): lax.psum_scatter(column_terms(weights, row_block), 'outer', scatter_dimen...  22.5 us
    psum x1, blocking collectives, shards(): row_total = lax.psum(jnp.sum(exponent, 1), 'inner')  19.2 us
    all_to_all x1, waiting for transfers between devices, shards(): lax.all_to_all(relayed, 'inner', split_axis=0, concat_axis=0, tiled=True)  8.87 us
    all_to_all x1, starting transfers between devices, shards(): lax.all_to_all(request_group, 'inner', split_axis=0, concat_axis=0, tiled...  7.28 us
    all_gather x1, blocking collectives, shards(): lax.all_gather(queries, 'outer', axis=0, tiled=True)  6.51 us
    all_to_all x1, waiting for transfers between devices, shards(): lax.all_to_all(looked, 'outer', split_axis=0, concat_axis=0, tiled=True)  5.99 us
    psum x1, blocking collectives, shards(): column_total = lax.psum(jnp.sum(exponent, 0), 'outer')  5.66 us
  transfers between devices with their start and end apart: 7, of which 7 were waited for; matrix products, arithmetic and copies ran while one was open for 2% of the time, Pallas kernels for 0%

commit v1 on v0

v1 whole, which is shorter than its diff:
```python
import functools

import jax
import jax.numpy as jnp
from jax import lax
from jax.experimental import pallas as pl
from jax.experimental.pallas import tpu as pltpu
from jax.sharding import PartitionSpec as P

EPS = 1e-06
INV_TAU = 10.0
MESH = pl.DeviceIdType.MESH
F32 = jnp.float32
BF16 = jnp.bfloat16


def kernel(
    outer, inner, cap,
    code_ref, pred_ref, queue_ref, out_ref,
    queue, gcodes, codes, places, queries, rows, ids, expo, row_sums, column_sums, partials, incoming,
    queue_sem, code_s, code_r, group_s, group_r, query_s, query_r,
    rows_s, rows_r, rsum_s, rsum_r, csum_s, csum_r, part_s, part_r,
):
    at_o = lax.axis_index("outer")
    at_i = lax.axis_index("inner")
    n, width = pred_ref.shape
    depth = queue_ref.shape[0]
    devices = outer * inner
    total_rows = outer * cap

    def inner_copy(src, dst, send, recv, peer):
        return pltpu.make_async_remote_copy(
            src_ref=src, dst_ref=dst, send_sem=send, recv_sem=recv,
            device_id=(at_o, peer), device_id_type=MESH,
        )

    def outer_copy(src, dst, send, recv, peer):
        return pltpu.make_async_remote_copy(
            src_ref=src, dst_ref=dst, send_sem=send, recv_sem=recv,
            device_id=(peer, at_i), device_id_type=MESH,
        )

    def each_inner(body):
        def step(k, carry):
            body(lax.rem(at_i + k, inner))
            return carry

        lax.fori_loop(1, inner, step, 0)

    def each_outer(body):
        for k in range(1, outer):
            body(lax.rem(at_o + k, outer))

    load_queue = pltpu.make_async_copy(queue_ref, queue, queue_sem)
    load_queue.start()

    barrier = pltpu.get_barrier_semaphore()
    each_inner(lambda p: pl.semaphore_signal(barrier, inc=1, device_id=(at_o, p), device_id_type=MESH))
    each_outer(lambda p: pl.semaphore_signal(barrier, inc=1, device_id=(p, at_i), device_id_type=MESH))

    gcodes[at_o, at_i] = code_ref[...]
    predicted = pred_ref[...].astype(F32)
    inverse = lax.rsqrt(jnp.sum(predicted * predicted, 1, keepdims=True) + EPS)
    queries[at_i] = (predicted * inverse).astype(BF16)

    pl.semaphore_wait(barrier, inner + outer - 2)

    def code_copy(slot, peer):
        return inner_copy(gcodes.at[at_o, slot], gcodes.at[at_o, slot], code_s.at[peer], code_r.at[slot], peer)

    def query_copy(slot, peer):
        return inner_copy(queries.at[slot], queries.at[slot], query_s.at[peer], query_r.at[slot], peer)

    def group_copy(slot, peer):
        return outer_copy(gcodes.at[slot], gcodes.at[slot], group_s.at[peer], group_r.at[slot], peer)

    def rows_copy(slot, peer):
        return outer_copy(rows.at[slot], rows.at[slot], rows_s.at[peer], rows_r.at[slot], peer)

    def rsum_copy(slot, peer):
        return outer_copy(row_sums.at[slot], row_sums.at[slot], rsum_s.at[peer], rsum_r.at[slot], peer)

    def csum_copy(slot, peer):
        return inner_copy(column_sums.at[slot], column_sums.at[slot], csum_s.at[peer], csum_r.at[slot], peer)

    def part_copy(slot, peer):
        return inner_copy(partials.at[peer], incoming.at[slot], part_s.at[peer], part_r.at[slot], peer)

    each_inner(lambda p: code_copy(at_i, p).start())
    each_inner(lambda p: query_copy(at_i, p).start())
    each_inner(lambda p: code_copy(p, p).wait_recv())
    each_outer(lambda p: group_copy(at_o, p).start())
    each_outer(lambda p: group_copy(p, p).wait_recv())

    def unpack(r, carry):
        codes[pl.ds(r, 1), :] = gcodes[r // inner, lax.rem(r, inner)]
        return carry

    lax.fori_loop(0, devices, unpack, 0)

    lane_from = lax.broadcasted_iota(jnp.int32, (n, n), 0)
    lane_to = lax.broadcasted_iota(jnp.int32, (n, n), 1)
    before_lane = (lane_from < lane_to).astype(BF16)
    ones = jnp.ones((n, n), BF16)
    row_to = lax.broadcasted_iota(jnp.int32, (devices, devices), 0)
    row_from = lax.broadcasted_iota(jnp.int32, (devices, devices), 1)
    before_row = (row_from < row_to).astype(BF16)
    place_iota = lax.broadcasted_iota(jnp.int32, (cap, n), 0)
    lanes = lax.broadcasted_iota(jnp.int32, (1, n), 1)

    def compact(device):
        mask = (codes[...] // depth) == device
        hits = mask.astype(F32).astype(BF16)
        in_row = jnp.dot(hits, before_lane, preferred_element_type=F32)
        counts = jnp.dot(hits, ones, preferred_element_type=F32).astype(BF16)
        above = jnp.dot(before_row, counts, preferred_element_type=F32)
        places[...] = jnp.where(mask, (in_row + above).astype(jnp.int32), -1)

        def step(r, found):
            entry = (r * n + lanes + 1) * depth + lax.rem(codes[pl.ds(r, 1), :], depth)
            return found + jnp.where(places[pl.ds(r, 1), :] == place_iota, entry, 0)

        return lax.fori_loop(0, devices, step, jnp.zeros((cap, n), jnp.int32), unroll=4)

    found = compact(at_o * inner + at_i)
    slot = jnp.sum(lax.rem(found, depth).astype(F32), 1, keepdims=True)
    named = jnp.sum((found // depth).astype(F32), 1, keepdims=True)
    slot = jnp.where(named > 0.5, slot, -1.0).astype(jnp.int32)

    load_queue.wait()
    chunk = min(512, depth)
    chunk_iota = lax.broadcasted_iota(jnp.int32, (cap, chunk), 1)

    def look(c, total):
        start = pl.multiple_of(c * chunk, chunk)
        pick = (slot - start == chunk_iota).astype(F32).astype(BF16)
        return total + jnp.dot(pick, queue[pl.ds(start, chunk), :], preferred_element_type=F32)

    fetched = lax.fori_loop(0, depth // chunk, look, jnp.zeros((cap, width), F32))
    scale = lax.rsqrt(jnp.sum(fetched * fetched, 1, keepdims=True) + EPS)
    rows[at_o] = (fetched * scale).astype(BF16)
    each_outer(lambda p: rows_copy(at_o, p).start())

    for a in range(outer):
        found = compact(a * inner + at_i)
        ids[:, a * cap:(a + 1) * cap] = (
            jnp.sum(jnp.transpose((found // depth).astype(F32)), 0, keepdims=True) - 1.0
        )
    row_sums[at_o] = jnp.zeros((1, total_rows), F32)
    each_outer(lambda p: rows_copy(p, p).wait_recv())

    def score(m):
        row_part = []
        column_part = jnp.zeros((n, n), F32)
        for a in range(outer):
            valid = (ids[:, a * cap:(a + 1) * cap] > -0.5).astype(F32)
            e = jnp.exp(
                lax.dot_general(
                    queries[m], rows[a], (((1,), (1,)), ((), ())), preferred_element_type=F32
                ) * INV_TAU
            ) * valid
            expo[m, :, a * cap:(a + 1) * cap] = e.astype(expo.dtype)
            row_part.append(jnp.sum(e, 0, keepdims=True))
            for b in range(0, cap, n):
                column_part = column_part + e[:, b:b + n]
        row_sums[at_o] = row_sums[at_o] + jnp.concatenate(row_part, 1)
        column_sums[at_i, pl.ds(m, 1), :] = jnp.sum(jnp.transpose(column_part), 0, keepdims=True)

    score(at_i)

    def score_peer(p):
        query_copy(p, p).wait_recv()
        score(p)

    each_inner(score_peer)

    each_inner(lambda p: csum_copy(at_i, p).start())
    each_outer(lambda p: rsum_copy(at_o, p).start())
    each_outer(lambda p: rsum_copy(p, p).wait_recv())
    row_total = row_sums[0]
    for a in range(1, outer):
        row_total = row_total + row_sums[a]
    valid = ids[...] > -0.5
    row_scale = jnp.where(valid, 0.5 / jnp.where(valid, row_total, 1.0), 0.0)
    each_inner(lambda p: csum_copy(p, p).wait_recv())

    def add_columns(s, total):
        return total + column_sums[s]

    column_total = lax.fori_loop(0, inner, add_columns, jnp.zeros((inner, n), F32))
    column_scales = 0.5 / column_total

    def gradient(m):
        pick = lax.broadcasted_iota(jnp.int32, (inner, n), 0) == m
        scale_row = jnp.sum(jnp.where(pick, column_scales, 0.0), 0, keepdims=True)
        column_scale = jnp.transpose(jnp.broadcast_to(scale_row, (n, n)))[:, :1]
        first = ((at_o * inner + m) * n).astype(F32)
        column_ids = lax.broadcasted_iota(jnp.int32, (n, 1), 0).astype(F32) + first
        total = jnp.zeros((n, width), F32)
        for a in range(outer):
            span = slice(a * cap, (a + 1) * cap)
            e = expo[m, :, span].astype(F32)
            diagonal = (ids[:, span] == column_ids).astype(F32)
            weights = (e * (row_scale[:, span] + column_scale) - diagonal).astype(BF16)
            total = total + jnp.dot(weights, rows[a], preferred_element_type=F32)
        return total

    def gradient_peer(p):
        partials[p] = gradient(p).astype(BF16)
        part_copy(at_i, p).start()

    each_inner(gradient_peer)
    out_ref[...] = gradient(at_i)

    def collect(p):
        part_copy(p, p).wait_recv()
        out_ref[...] = out_ref[...] + incoming[p].astype(F32)

    each_inner(collect)
    dquery = out_ref[...] * INV_TAU
    radial = jnp.sum(predicted * dquery, 1, keepdims=True)
    out_ref[...] = inverse * dquery - predicted * inverse * inverse * inverse * radial

    def drain_inner(p):
        code_copy(at_i, p).wait_send()
        query_copy(at_i, p).wait_send()
        csum_copy(at_i, p).wait_send()
        part_copy(at_i, p).wait_send()

    each_inner(drain_inner)

    def drain_outer(p):
        group_copy(at_o, p).wait_send()
        rows_copy(at_o, p).wait_send()
        rsum_copy(at_o, p).wait_send()

    each_outer(drain_outer)


def shards(queue, pred, owner, slot):
    outer = lax.axis_size("outer")
    inner = lax.axis_size("inner")
    n, width = pred.shape
    depth = queue.shape[0]
    cap = inner * max(2, 2 * n // inner)
    total_rows = outer * cap
    expo_type = F32 if inner * n * total_rows * 4 <= 2**23 else BF16
    code = (owner[:, 0] * depth + slot).reshape(1, n)
    dma = pltpu.SemaphoreType.DMA
    vmem = pltpu.VMEM
    return pl.pallas_call(
        functools.partial(kernel, outer, inner, cap),
        out_shape=jax.ShapeDtypeStruct((n, width), F32),
        in_specs=[
            pl.BlockSpec(memory_space=vmem),
            pl.BlockSpec(memory_space=vmem),
            pl.BlockSpec(memory_space=pl.ANY),
        ],
        out_specs=pl.BlockSpec(memory_space=vmem),
        scratch_shapes=[
            vmem((depth, width), BF16),
            vmem((outer, inner, 1, n), jnp.int32),
            vmem((outer * inner, n), jnp.int32),
            vmem((outer * inner, n), jnp.int32),
            vmem((inner, n, width), BF16),
            vmem((outer, cap, width), BF16),
            vmem((1, total_rows), F32),
            vmem((inner, n, total_rows), expo_type),
            vmem((outer, 1, total_rows), F32),
            vmem((inner, inner, n), F32),
            vmem((inner, n, width), BF16),
            vmem((inner, n, width), BF16),
            dma,
            dma((inner,)), dma((inner,)),
            dma((outer,)), dma((outer,)),
            dma((inner,)), dma((inner,)),
            dma((outer,)), dma((outer,)),
            dma((outer,)), dma((outer,)),
            dma((inner,)), dma((inner,)),
            dma((inner,)), dma((inner,)),
        ],
        compiler_params=pltpu.CompilerParams(
            collective_id=0, has_side_effects=True, vmem_limit_bytes=58 * 2**20
        ),
    )(code, pred, queue)


def solution(mesh):
    in_specs = (
        P(("outer", "inner"), None),
        P(("outer", "inner"), None),
        P(("outer", "inner"), None),
        P(("outer", "inner")),
    )
    out_specs = P(("outer", "inner"), None)
    return jax.shard_map(shards, mesh=mesh, in_specs=in_specs, out_specs=out_specs, check_vma=False)
```

time: 178 us -> 74.2 us (0.42)
  the two profiles are of different devices: /device:TPU:0 before, /device:TPU:29 now
where the time goes in v1:
time: 74.2 us; the launch traced here: 74 us
  Pallas kernels  71.2 us (96%)
  local copies, waits for them, and re-layouts  1.67 us (2%)
  other arithmetic  1.18 us (2%)
    pallas_call x1, Pallas kernels, shards(): pl.pallas_call(functools.partial(kernel, outer, inner, cap), out_shape=ja...  71.2 us
    unnamed x1, local copies, waits for them, and re-layouts  1.67 us

profile of v1, /device:TPU:29, one launch (start us, length us, event | category | flops | bytes accessed | tf_op | source)
XLA Modules:
  0.0 74.0 jit_solution(9029609358599723867)
XLA Ops:
  0.0 1.2 %fusion.code_ref = s32[1,128]{1,0:T(1,128)} fusion(s32[128]{0:T(128)} %param.7, s32[128,1]{0,1:T(1,128)} %param.6), kind=kLoop, calls=%fused_computation.1 | loop fusion | flops 256 | bytes 1536 | tf_op jit(solution)/shard_map/reshape | solution.py:248
  1.2 71.2 %shard_map.46 = f32[128,512]{1,0:T(8,128)} custom-call(s32[1,128]{1,0:T(1,128)} %fusion.code_ref, bf16[128,512]{1,0:T(8,128)(2,1)} %pred_ref.1, bf16[4096,512]{1,0:T(8,128)(2,1)} %queue_ref.1), custom_call_target="tpu_custom_call" | custom-call | tf_op jit(solution)/shard_map/pallas_call | solution.py:251
  72.4 1.7 %copy.6 = f32[128,512]{1,0:T(8,128)} copy(f32[128,512]{1,0:T(8,128)} %shard_map.46) | data formatting | bytes 524288

commit v2 on v1

--- a/solution.py
+++ b/solution.py
@@ -9,6 +9,7 @@
 
 EPS = 1e-06
 INV_TAU = 10.0
+PIECES = 4
 MESH = pl.DeviceIdType.MESH
 F32 = jnp.float32
 BF16 = jnp.bfloat16
@@ -19,7 +20,7 @@
     code_ref, pred_ref, queue_ref, out_ref,
     queue, gcodes, codes, places, queries, rows, ids, expo, row_sums, column_sums, partials, incoming,
     queue_sem, code_s, code_r, group_s, group_r, query_s, query_r,
-    rows_s, rows_r, rsum_s, rsum_r, csum_s, csum_r, part_s, part_r,
+    rows_s, rows_r, ids_s, ids_r, rsum_s, rsum_r, csum_s, csum_r, part_s, part_r,
 ):
     at_o = lax.axis_index("outer")
     at_i = lax.axis_index("inner")
@@ -27,6 +28,9 @@
     depth = queue_ref.shape[0]
     devices = outer * inner
     total_rows = outer * cap
+    piece = cap // PIECES
+    beside_o = at_o + 1 - 2 * lax.rem(at_o, 2)
+    beside_i = at_i + 1 - 2 * lax.rem(at_i, 2)
 
     def inner_copy(src, dst, send, recv, peer):
         return pltpu.make_async_remote_copy(
@@ -51,6 +55,20 @@
         for k in range(1, outer):
             body(lax.rem(at_o + k, outer))
 
+    def far_inner(body, start=at_i):
+        def step(k, carry):
+            body(lax.rem(start + 2 * k, inner))
+            return carry
+
+        lax.fori_loop(1, inner // 2, step, 0)
+
+    def far_outer(body):
+        for k in range(1, outer // 2):
+            body(lax.rem(at_o + 2 * k, outer))
+
+    def other(index):
+        return index + 1 - 2 * lax.rem(index, 2)
+
     load_queue = pltpu.make_async_copy(queue_ref, queue, queue_sem)
     load_queue.start()
 
@@ -68,14 +86,18 @@
     def code_copy(slot, peer):
         return inner_copy(gcodes.at[at_o, slot], gcodes.at[at_o, slot], code_s.at[peer], code_r.at[slot], peer)
 
-    def query_copy(slot, peer):
-        return inner_copy(queries.at[slot], queries.at[slot], query_s.at[peer], query_r.at[slot], peer)
+    def query_copy(slot, peer, lane):
+        return inner_copy(queries.at[slot], queries.at[slot], query_s.at[lane], query_r.at[slot], peer)
 
     def group_copy(slot, peer):
         return outer_copy(gcodes.at[slot], gcodes.at[slot], group_s.at[peer], group_r.at[slot], peer)
 
-    def rows_copy(slot, peer):
-        return outer_copy(rows.at[slot], rows.at[slot], rows_s.at[peer], rows_r.at[slot], peer)
+    def rows_copy(slot, c, peer, lane):
+        part = rows.at[slot, pl.ds(c * piece, piece)]
+        return outer_copy(part, part, rows_s.at[lane, c], rows_r.at[slot, c], peer)
+
+    def ids_copy(slot, peer):
+        return outer_copy(ids.at[slot], ids.at[slot], ids_s.at[peer], ids_r.at[slot], peer)
 
     def rsum_copy(slot, peer):
         return outer_copy(row_sums.at[slot], row_sums.at[slot], rsum_s.at[peer], rsum_r.at[slot], peer)
@@ -83,11 +105,12 @@
     def csum_copy(slot, peer):
         return inner_copy(column_sums.at[slot], column_sums.at[slot], csum_s.at[peer], csum_r.at[slot], peer)
 
-    def part_copy(slot, peer):
-        return inner_copy(partials.at[peer], incoming.at[slot], part_s.at[peer], part_r.at[slot], peer)
+    def part_copy(block, slot, peer):
+        return inner_copy(partials.at[block], incoming.at[slot], part_s.at[block], part_r.at[slot], peer)
 
     each_inner(lambda p: code_copy(at_i, p).start())
-    each_inner(lambda p: query_copy(at_i, p).start())
+    far_inner(lambda p: query_copy(at_i, p, p).start())
+    query_copy(at_i, beside_i, beside_i).start()
     each_inner(lambda p: code_copy(p, p).wait_recv())
     each_outer(lambda p: group_copy(at_o, p).start())
     each_outer(lambda p: group_copy(p, p).wait_recv())
@@ -139,21 +162,36 @@
     fetched = lax.fori_loop(0, depth // chunk, look, jnp.zeros((cap, width), F32))
     scale = lax.rsqrt(jnp.sum(fetched * fetched, 1, keepdims=True) + EPS)
     rows[at_o] = (fetched * scale).astype(BF16)
-    each_outer(lambda p: rows_copy(at_o, p).start())
-
-    for a in range(outer):
-        found = compact(a * inner + at_i)
-        ids[:, a * cap:(a + 1) * cap] = (
-            jnp.sum(jnp.transpose((found // depth).astype(F32)), 0, keepdims=True) - 1.0
-        )
+    for c in range(PIECES):
+        far_outer(lambda p: rows_copy(at_o, c, p, p).start())
+    for c in range(PIECES):
+        rows_copy(at_o, c, beside_o, beside_o).start()
+    ids[at_o] = jnp.sum(jnp.transpose((found // depth).astype(F32)), 0, keepdims=True) - 1.0
+    each_outer(lambda p: ids_copy(at_o, p).start())
     row_sums[at_o] = jnp.zeros((1, total_rows), F32)
-    each_outer(lambda p: rows_copy(p, p).wait_recv())
+
+    def forward_query(p):
+        query_copy(p, p, p).wait_recv()
+        query_copy(p, beside_i, other(p)).start()
+
+    far_inner(forward_query)
+    for c in range(PIECES):
+
+        def forward_rows(p):
+            rows_copy(p, c, p, p).wait_recv()
+            rows_copy(p, c, beside_o, other(p)).start()
+
+        far_outer(forward_rows)
+    each_outer(lambda p: ids_copy(p, p).wait_recv())
+    for c in range(PIECES):
+        rows_copy(beside_o, c, beside_o, beside_o).wait_recv()
+        far_outer(lambda p: rows_copy(other(p), c, beside_o, beside_o).wait_recv())
 
     def score(m):
         row_part = []
         column_part = jnp.zeros((n, n), F32)
         for a in range(outer):
-            valid = (ids[:, a * cap:(a + 1) * cap] > -0.5).astype(F32)
+            valid = (ids[a] > -0.5).astype(F32)
             e = jnp.exp(
                 lax.dot_general(
                     queries[m], rows[a], (((1,), (1,)), ((), ())), preferred_element_type=F32
@@ -167,12 +205,14 @@
         column_sums[at_i, pl.ds(m, 1), :] = jnp.sum(jnp.transpose(column_part), 0, keepdims=True)
 
     score(at_i)
+    far_inner(score)
 
     def score_peer(p):
-        query_copy(p, p).wait_recv()
+        query_copy(p, p, p).wait_recv()
         score(p)
 
-    each_inner(score_peer)
+    score_peer(beside_i)
+    far_inner(score_peer, beside_i)
 
     each_inner(lambda p: csum_copy(at_i, p).start())
     each_outer(lambda p: rsum_copy(at_o, p).start())
@@ -180,7 +220,7 @@
     row_total = row_sums[0]
     for a in range(1, outer):
         row_total = row_total + row_sums[a]
-    valid = ids[...] > -0.5
+    valid = jnp.concatenate([ids[a] for a in range(outer)], 1) > -0.5
     row_scale = jnp.where(valid, 0.5 / jnp.where(valid, row_total, 1.0), 0.0)
     each_inner(lambda p: csum_copy(p, p).wait_recv())
 
@@ -200,38 +240,50 @@
         for a in range(outer):
             span = slice(a * cap, (a + 1) * cap)
             e = expo[m, :, span].astype(F32)
-            diagonal = (ids[:, span] == column_ids).astype(F32)
+            diagonal = (ids[a] == column_ids).astype(F32)
             weights = (e * (row_scale[:, span] + column_scale) - diagonal).astype(BF16)
             total = total + jnp.dot(weights, rows[a], preferred_element_type=F32)
         return total
 
-    def gradient_peer(p):
+    def gradient_beside(p):
         partials[p] = gradient(p).astype(BF16)
-        part_copy(at_i, p).start()
-
-    each_inner(gradient_peer)
+        part_copy(p, p, beside_i).start()
+
+    far_inner(gradient_beside, beside_i)
+    gradient_beside(beside_i)
     out_ref[...] = gradient(at_i)
 
-    def collect(p):
-        part_copy(p, p).wait_recv()
-        out_ref[...] = out_ref[...] + incoming[p].astype(F32)
-
-    each_inner(collect)
+    def gradient_far(p):
+        own = gradient(p)
+        part_copy(p, p, p).wait_recv()
+        partials[p] = (own + incoming[p].astype(F32)).astype(BF16)
+        part_copy(p, beside_i, p).start()
+
+    far_inner(gradient_far)
+
+    def collect(slot):
+        part_copy(slot, slot, beside_i).wait_recv()
+        out_ref[...] = out_ref[...] + incoming[slot].astype(F32)
+
+    collect(at_i)
+    far_inner(lambda p: collect(other(p)))
     dquery = out_ref[...] * INV_TAU
     radial = jnp.sum(predicted * dquery, 1, keepdims=True)
     out_ref[...] = inverse * dquery - predicted * inverse * inverse * inverse * radial
 
     def drain_inner(p):
         code_copy(at_i, p).wait_send()
-        query_copy(at_i, p).wait_send()
+        query_copy(at_i, beside_i, p).wait_send()
         csum_copy(at_i, p).wait_send()
-        part_copy(at_i, p).wait_send()
+        part_copy(p, p, beside_i).wait_send()
 
     each_inner(drain_inner)
 
     def drain_outer(p):
         group_copy(at_o, p).wait_send()
-        rows_copy(at_o, p).wait_send()
+        for c in range(PIECES):
+            rows_copy(at_o, c, beside_o, p).wait_send()
+        ids_copy(at_o, p).wait_send()
         rsum_copy(at_o, p).wait_send()
 
     each_outer(drain_outer)
@@ -264,7 +316,7 @@
             vmem((outer * inner, n), jnp.int32),
             vmem((inner, n, width), BF16),
             vmem((outer, cap, width), BF16),
-            vmem((1, total_rows), F32),
+            vmem((outer, 1, cap), F32),
             vmem((inner, n, total_rows), expo_type),
             vmem((outer, 1, total_rows), F32),
             vmem((inner, inner, n), F32),
@@ -274,6 +326,7 @@
             dma((inner,)), dma((inner,)),
             dma((outer,)), dma((outer,)),
             dma((inner,)), dma((inner,)),
+            dma((outer, PIECES)), dma((outer, PIECES)),
             dma((outer,)), dma((outer,)),
             dma((outer,)), dma((outer,)),
             dma((inner,)), dma((inner,)),

time: 74.2 us -> 59.8 us (0.81)
  the two profiles are of different devices: /device:TPU:29 before, /device:TPU:0 now
where the time goes in v2:
time: 59.8 us; the launch traced here: 59.7 us
  Pallas kernels  56.8 us (95%)
  local copies, waits for them, and re-layouts  1.67 us (3%)
  other arithmetic  1.18 us (2%)
    pallas_call x1, Pallas kernels, shards(): pl.pallas_call(functools.partial(kernel, outer, inner, cap), out_shape=ja...  56.8 us
    unnamed x1, local copies, waits for them, and re-layouts  1.67 us

profile of v2, /device:TPU:0, one launch (start us, length us, event | category | flops | bytes accessed | tf_op | source)
XLA Modules:
  0.0 59.7 jit_solution(2402229580676054763)
XLA Ops:
  0.0 1.2 %fusion.code_ref = s32[1,128]{1,0:T(1,128)} fusion(s32[128]{0:T(128)} %param.7, s32[128,1]{0,1:T(1,128)} %param.6), kind=kLoop, calls=%fused_computation.1 | loop fusion | flops 256 | bytes 1536 | tf_op jit(solution)/shard_map/reshape | solution.py:300
  1.2 56.8 %shard_map.46 = f32[128,512]{1,0:T(8,128)} custom-call(s32[1,128]{1,0:T(1,128)} %fusion.code_ref, bf16[128,512]{1,0:T(8,128)(2,1)} %pred_ref.1, bf16[4096,512]{1,0:T(8,128)(2,1)} %queue_ref.1), custom_call_target="tpu_custom_call" | custom-call | tf_op jit(solution)/shard_map/pallas_call | solution.py:303
  58.0 1.7 %copy.6 = f32[128,512]{1,0:T(8,128)} copy(f32[128,512]{1,0:T(8,128)} %shard_map.46) | data formatting | bytes 524288

commit v3 on v2

--- a/solution.py
+++ b/solution.py
@@ -17,7 +17,7 @@
 
 def kernel(
     outer, inner, cap,
-    code_ref, pred_ref, queue_ref, out_ref,
+    owner_ref, slot_ref, pred_ref, queue_ref, out_ref,
     queue, gcodes, codes, places, queries, rows, ids, expo, row_sums, column_sums, partials, incoming,
     queue_sem, code_s, code_r, group_s, group_r, query_s, query_r,
     rows_s, rows_r, ids_s, ids_r, rsum_s, rsum_r, csum_s, csum_r, part_s, part_r,
@@ -76,7 +76,7 @@
     each_inner(lambda p: pl.semaphore_signal(barrier, inc=1, device_id=(at_o, p), device_id_type=MESH))
     each_outer(lambda p: pl.semaphore_signal(barrier, inc=1, device_id=(p, at_i), device_id_type=MESH))
 
-    gcodes[at_o, at_i] = code_ref[...]
+    gcodes[at_o, at_i] = owner_ref[...] * depth + slot_ref[...]
     predicted = pred_ref[...].astype(F32)
     inverse = lax.rsqrt(jnp.sum(predicted * predicted, 1, keepdims=True) + EPS)
     queries[at_i] = (predicted * inverse).astype(BF16)
@@ -151,7 +151,7 @@
     slot = jnp.where(named > 0.5, slot, -1.0).astype(jnp.int32)
 
     load_queue.wait()
-    chunk = min(512, depth)
+    chunk = min(2048, depth)
     chunk_iota = lax.broadcasted_iota(jnp.int32, (cap, chunk), 1)
 
     def look(c, total):
@@ -159,7 +159,7 @@
         pick = (slot - start == chunk_iota).astype(F32).astype(BF16)
         return total + jnp.dot(pick, queue[pl.ds(start, chunk), :], preferred_element_type=F32)
 
-    fetched = lax.fori_loop(0, depth // chunk, look, jnp.zeros((cap, width), F32))
+    fetched = lax.fori_loop(0, depth // chunk, look, jnp.zeros((cap, width), F32), unroll=True)
     scale = lax.rsqrt(jnp.sum(fetched * fetched, 1, keepdims=True) + EPS)
     rows[at_o] = (fetched * scale).astype(BF16)
     for c in range(PIECES):
@@ -297,13 +297,13 @@
     cap = inner * max(2, 2 * n // inner)
     total_rows = outer * cap
     expo_type = F32 if inner * n * total_rows * 4 <= 2**23 else BF16
-    code = (owner[:, 0] * depth + slot).reshape(1, n)
     dma = pltpu.SemaphoreType.DMA
     vmem = pltpu.VMEM
     return pl.pallas_call(
         functools.partial(kernel, outer, inner, cap),
         out_shape=jax.ShapeDtypeStruct((n, width), F32),
         in_specs=[
+            pl.BlockSpec(memory_space=vmem),
             pl.BlockSpec(memory_space=vmem),
             pl.BlockSpec(memory_space=vmem),
             pl.BlockSpec(memory_space=pl.ANY),
@@ -335,7 +335,7 @@
         compiler_params=pltpu.CompilerParams(
             collective_id=0, has_side_effects=True, vmem_limit_bytes=58 * 2**20
         ),
-    )(code, pred, queue)
+    )(owner.reshape(1, n), slot.reshape(1, n), pred, queue)
 
 
 def solution(mesh):

time: 59.8 us -> 57.1 us (0.955)
  Pallas kernels: 56.8 us -> 55.2 us
  other arithmetic: 1.18 us -> 0 us
    pallas_call x1, Pallas kernels: 56.8 us -> 55.2 us  [shards(): pl.pallas_call(functools.partial(kernel, outer, inner, cap), out_shape=ja...]
    reshape x1 -> x0, other arithmetic: 1.18 us -> none  [shards(): code = (owner[:, 0] * depth + slot).reshape(1, n)]
where the time goes in v3:
time: 57.1 us; the launch traced here: 56.9 us
  Pallas kernels  55.2 us (97%)
  local copies, waits for them, and re-layouts  1.67 us (3%)
    pallas_call x1, Pallas kernels, shards(): pl.pallas_call(functools.partial(kernel, outer, inner, cap), out_shape=ja...  55.2 us
    unnamed x1, local copies, waits for them, and re-layouts  1.67 us

profile of v3, /device:TPU:0, one launch (start us, length us, event | category | flops | bytes accessed | tf_op | source)
XLA Modules:
  0.0 56.9 jit_solution(13325833868532021816)
XLA Ops:
  0.0 55.2 %shard_map.46 = f32[128,512]{1,0:T(8,128)} custom-call(s32[1,128]{1,0:T(1,128)} %bitcast.2, s32[1,128]{1,0:T(1,128)} %bitcast.3, bf16[128,512]{1,0:T(8,128)(2,1)} %pred_ref.1, bf16[4096,512]{1,0:T(8,128)(2,1)} %queue_ref.1), custom_call_target="tpu_custom_call" | custom-call | tf_op jit(solution)/shard_map/pallas_call | solution.py:302
  55.2 1.7 %copy.6 = f32[128,512]{1,0:T(8,128)} copy(f32[128,512]{1,0:T(8,128)} %shard_map.46) | data formatting | bytes 524288

commit v4 on v3

--- a/solution.py
+++ b/solution.py
@@ -105,8 +105,12 @@
     def csum_copy(slot, peer):
         return inner_copy(column_sums.at[slot], column_sums.at[slot], csum_s.at[peer], csum_r.at[slot], peer)
 
-    def part_copy(block, slot, peer):
-        return inner_copy(partials.at[block], incoming.at[slot], part_s.at[block], part_r.at[slot], peer)
+    def part_copy(block, slot, peer, half):
+        span = pl.ds(half * (n // 2), n // 2)
+        return inner_copy(
+            partials.at[block, span], incoming.at[slot, span],
+            part_s.at[block, half], part_r.at[slot, half], peer,
+        )
 
     each_inner(lambda p: code_copy(at_i, p).start())
     far_inner(lambda p: query_copy(at_i, p, p).start())
@@ -187,32 +191,38 @@
         rows_copy(beside_o, c, beside_o, beside_o).wait_recv()
         far_outer(lambda p: rows_copy(other(p), c, beside_o, beside_o).wait_recv())
 
+    wide = 4 if inner % 4 == 0 else 1
+
     def score(m):
         row_part = []
-        column_part = jnp.zeros((n, n), F32)
+        column_part = jnp.zeros((wide * n, n), F32)
+        block = queries[pl.ds(m * wide, wide)].reshape(wide * n, width)
         for a in range(outer):
             valid = (ids[a] > -0.5).astype(F32)
             e = jnp.exp(
                 lax.dot_general(
-                    queries[m], rows[a], (((1,), (1,)), ((), ())), preferred_element_type=F32
+                    block, rows[a], (((1,), (1,)), ((), ())), preferred_element_type=F32
                 ) * INV_TAU
             ) * valid
-            expo[m, :, a * cap:(a + 1) * cap] = e.astype(expo.dtype)
+            for j in range(wide):
+                expo[m * wide + j, :, a * cap:(a + 1) * cap] = e[j * n:(j + 1) * n].astype(expo.dtype)
             row_part.append(jnp.sum(e, 0, keepdims=True))
             for b in range(0, cap, n):
                 column_part = column_part + e[:, b:b + n]
         row_sums[at_o] = row_sums[at_o] + jnp.concatenate(row_part, 1)
-        column_sums[at_i, pl.ds(m, 1), :] = jnp.sum(jnp.transpose(column_part), 0, keepdims=True)
-
-    score(at_i)
-    far_inner(score)
-
-    def score_peer(p):
-        query_copy(p, p, p).wait_recv()
-        score(p)
-
-    score_peer(beside_i)
-    far_inner(score_peer, beside_i)
+        for j in range(wide):
+            column_sums[at_i, pl.ds(m * wide + j, 1), :] = jnp.sum(
+                jnp.transpose(column_part[j * n:(j + 1) * n]), 0, keepdims=True
+            )
+
+    query_copy(beside_i, beside_i, beside_i).wait_recv()
+    far_inner(lambda p: query_copy(p, p, p).wait_recv(), beside_i)
+
+    def score_step(m, carry):
+        score(m)
+        return carry
+
+    lax.fori_loop(0, inner // wide, score_step, 0)
 
     each_inner(lambda p: csum_copy(at_i, p).start())
     each_outer(lambda p: rsum_copy(at_o, p).start())
@@ -247,7 +257,8 @@
 
     def gradient_beside(p):
         partials[p] = gradient(p).astype(BF16)
-        part_copy(p, p, beside_i).start()
+        for half in range(2):
+            part_copy(p, p, beside_i, half).start()
 
     far_inner(gradient_beside, beside_i)
     gradient_beside(beside_i)
@@ -255,14 +266,17 @@
 
     def gradient_far(p):
         own = gradient(p)
-        part_copy(p, p, p).wait_recv()
-        partials[p] = (own + incoming[p].astype(F32)).astype(BF16)
-        part_copy(p, beside_i, p).start()
+        for half in range(2):
+            span = slice(half * (n // 2), (half + 1) * (n // 2))
+            part_copy(p, p, p, half).wait_recv()
+            partials[p, span] = (own[span] + incoming[p, span].astype(F32)).astype(BF16)
+            part_copy(p, beside_i, p, half).start()
 
     far_inner(gradient_far)
 
     def collect(slot):
-        part_copy(slot, slot, beside_i).wait_recv()
+        for half in range(2):
+            part_copy(slot, slot, beside_i, half).wait_recv()
         out_ref[...] = out_ref[...] + incoming[slot].astype(F32)
 
     collect(at_i)
@@ -275,7 +289,8 @@
         code_copy(at_i, p).wait_send()
         query_copy(at_i, beside_i, p).wait_send()
         csum_copy(at_i, p).wait_send()
-        part_copy(p, p, beside_i).wait_send()
+        for half in range(2):
+            part_copy(p, p, beside_i, half).wait_send()
 
     each_inner(drain_inner)
 
@@ -330,7 +345,7 @@
             dma((outer,)), dma((outer,)),
             dma((outer,)), dma((outer,)),
             dma((inner,)), dma((inner,)),
-            dma((inner,)), dma((inner,)),
+            dma((inner, 2)), dma((inner, 2)),
         ],
         compiler_params=pltpu.CompilerParams(
             collective_id=0, has_side_effects=True, vmem_limit_bytes=58 * 2**20

time: 57.1 us -> 54.5 us (0.954)
  Pallas kernels: 55.2 us -> 52.6 us
    pallas_call x1, Pallas kernels: 55.2 us -> 52.6 us  [shards(): pl.pallas_call(functools.partial(kernel, outer, inner, cap), out_shape=ja...]
where the time goes in v4:
time: 54.5 us; the launch traced here: 54.3 us
  Pallas kernels  52.6 us (97%)
  local copies, waits for them, and re-layouts  1.67 us (3%)
    pallas_call x1, Pallas kernels, shards(): pl.pallas_call(functools.partial(kernel, outer, inner, cap), out_shape=ja...  52.6 us
    unnamed x1, local copies, waits for them, and re-layouts  1.67 us

profile of v4, /device:TPU:0, one launch (start us, length us, event | category | flops | bytes accessed | tf_op | source)
XLA Modules:
  0.0 54.3 jit_solution(2872938604618144079)
XLA Ops:
  0.0 52.6 %shard_map.46 = f32[128,512]{1,0:T(8,128)} custom-call(s32[1,128]{1,0:T(1,128)} %bitcast.2, s32[1,128]{1,0:T(1,128)} %bitcast.3, bf16[128,512]{1,0:T(8,128)(2,1)} %pred_ref.1, bf16[4096,512]{1,0:T(8,128)(2,1)} %queue_ref.1), custom_call_target="tpu_custom_call" | custom-call | tf_op jit(solution)/shard_map/pallas_call | solution.py:317
  52.7 1.7 %copy.6 = f32[128,512]{1,0:T(8,128)} copy(f32[128,512]{1,0:T(8,128)} %shard_map.46) | data formatting | bytes 524288

commit v5 on v4

--- a/solution.py
+++ b/solution.py
@@ -9,7 +9,7 @@
 
 EPS = 1e-06
 INV_TAU = 10.0
-PIECES = 4
+PIECES = 8
 MESH = pl.DeviceIdType.MESH
 F32 = jnp.float32
 BF16 = jnp.bfloat16
@@ -155,7 +155,7 @@
     slot = jnp.where(named > 0.5, slot, -1.0).astype(jnp.int32)
 
     load_queue.wait()
-    chunk = min(2048, depth)
+    chunk = min(4096, depth)
     chunk_iota = lax.broadcasted_iota(jnp.int32, (cap, chunk), 1)
 
     def look(c, total):

time: 54.5 us -> 54.9 us (level)
  no operation moved by 1% of the time
where the time goes in v5:
time: 54.9 us; the launch traced here: 54.7 us
  Pallas kernels  53 us (97%)
  local copies, waits for them, and re-layouts  1.67 us (3%)
    pallas_call x1, Pallas kernels, shards(): pl.pallas_call(functools.partial(kernel, outer, inner, cap), out_shape=ja...  53 us
    unnamed x1, local copies, waits for them, and re-layouts  1.67 us

profile of v5, /device:TPU:0, one launch (start us, length us, event | category | flops | bytes accessed | tf_op | source)
XLA Modules:
  0.0 54.7 jit_solution(5512041722028634940)
XLA Ops:
  0.0 53.0 %shard_map.46 = f32[128,512]{1,0:T(8,128)} custom-call(s32[1,128]{1,0:T(1,128)} %bitcast.2, s32[1,128]{1,0:T(1,128)} %bitcast.3, bf16[128,512]{1,0:T(8,128)(2,1)} %pred_ref.1, bf16[4096,512]{1,0:T(8,128)(2,1)} %queue_ref.1), custom_call_target="tpu_custom_call" | custom-call | tf_op jit(solution)/shard_map/pallas_call | solution.py:317
  53.0 1.7 %copy.6 = f32[128,512]{1,0:T(8,128)} copy(f32[128,512]{1,0:T(8,128)} %shard_map.46) | data formatting | bytes 524288
